TPU v7x, 32 devices: a whole 2x2x4 slice. The times are simulated.
32 devices in a mesh: bend: 2 (over core), head: 4 (over z), blk: 4 (over y, x).
Axes of the slice: x: 2, y: 2, z: 4, core: 2. Of those that a mesh axis runs over, the one named last changes fastest.
Arguments:
- queries: bfloat16 [4096, 1024], P(('bend', 'head', 'blk')), parts along dimension 0, may hold values from -6 to 6
- keys_in: bfloat16 [4096, 1024], P(('bend', 'head', 'blk')), parts along dimension 0, may hold values from -6 to 6
- values: bfloat16 [4096, 1024], P(('bend', 'head', 'blk')), parts along dimension 0, may hold values from -6 to 6
- d_out: bfloat16 [4096, 1024], P(('bend', 'head', 'blk')), parts along dimension 0, may hold values from -6 to 6
- token_count: int32 [2], P('bend'), parts along dimension 0, may hold values from 1024 to 2048
- block_ids: int32 [32], P('bend'), parts along dimension 0, may hold values from 0 to 15, each once
- neighbours: int32 [32, 10], P('bend'), parts along dimension 0, may hold values from 0 to 15, as said below
Outputs:
- grad_queries: bfloat16 [4096, 1024], P(('bend', 'head', 'blk')), parts along dimension 0
- grad_keys: bfloat16 [4096, 1024], P(('bend', 'head', 'blk')), parts along dimension 0
- grad_values: bfloat16 [4096, 1024], P(('bend', 'head', 'blk')), parts along dimension 0
There are 2 independent parts, one for each index of `bend`. A program takes and returns all parts, laid end to end along the dimension named above; each array names one. Nothing has to cross between parts.
Inputs may be any that keep to these rules, and one draw needn't show every extreme that they name: `neighbours`: column 0 of a row is the query block itself; the 10 entries of a row are distinct; every block appears in exactly 10 rows.
All inputs are finite; a program needn't handle non-finite values.
Results may differ from a plain program's by a relative error of at most 0.017.
Values may be sent and summed in bfloat16 or wider, within the bound.
A program may use at most 128 MiB of HBM per device.

v0:
```python
import math

import jax
import jax.numpy as jnp
from jax import lax
from jax.sharding import PartitionSpec as P

HD = 64
BLK = 128


neg_fill = -1e30
row_target = 512


def lookup(entries, wanted):
    matches = wanted[..., None] == jnp.arange(entries.shape[0], dtype=jnp.int32)
    return jnp.sum(jnp.where(matches, entries, 0), axis=-1)


def lookup_rows(entries, wanted):
    matches = wanted[..., None] == jnp.arange(entries.shape[0], dtype=jnp.int32)
    return jnp.sum(jnp.where(matches[..., None], entries, 0), axis=-2)


def group_size(blocks, block_rows):
    target = max(1, min(blocks, row_target // block_rows))
    while blocks % target != 0:
        target = target - 1
    return target


def block_tables(block_ids, neighbours, blk_count, head_count, block_rows, shard_rows):
    per_shard = shard_rows // block_rows
    local_blocks = head_count * per_shard
    slot_ids = jnp.arange(blk_count * local_blocks, dtype=jnp.int32)
    source = slot_ids // local_blocks
    within = slot_ids % local_blocks
    stored = (within // per_shard * blk_count + source) * per_shard + within % per_shard
    global_slot = lookup(block_ids, stored)
    matches = global_slot[None, :] == slot_ids[:, None]
    slot_global = jnp.sum(jnp.where(matches, slot_ids[None, :], 0), axis=1)
    key_global = lookup_rows(neighbours, global_slot)
    key_slots = lookup(slot_global, key_global)
    offsets = jnp.arange(block_rows, dtype=jnp.int32)
    query_where = global_slot[:, None] * block_rows + offsets
    key_where = key_global[:, :, None] * block_rows + offsets
    return (key_slots, query_where, key_where)


def permitted(query_where, key_where, token_limit):
    inside = key_where[:, None] < token_limit
    itself = key_where[:, None] == query_where[:, :, None, None]
    return inside | itself


def head_masks(feature_width, head_width):
    heads_here = feature_width // head_width
    owner_head = jnp.arange(feature_width, dtype=jnp.int32) // head_width
    return owner_head[None, :] == jnp.arange(heads_here, dtype=jnp.int32)[:, None]


def attend_all(query_tile, key_tile, value_tile, grad_tile, allowed, masks, score_scale):
    heads_here = masks.shape[0]
    query_sum = jnp.zeros(query_tile.shape, jnp.float32)
    key_sum = jnp.zeros(key_tile.shape, jnp.float32)
    value_sum = jnp.zeros(key_tile.shape, jnp.float32)
    logs = []
    deltas = []
    for head in range(heads_here):
        column_mask = masks[head]
        query_head = jnp.where(column_mask, query_tile, jnp.zeros_like(query_tile))
        grad_head = jnp.where(column_mask, grad_tile, jnp.zeros_like(grad_tile))
        product = (
            jnp.einsum("gqf,gnkf->gqnk", query_head, key_tile, preferred_element_type=jnp.float32)
            * score_scale
        )
        largest = jnp.max(jnp.where(allowed, product, neg_fill), axis=(2, 3), keepdims=True)
        denominator = jnp.sum(
            jnp.where(allowed, jnp.exp(product - largest), 0.0), axis=(2, 3), keepdims=True
        )
        log_total = largest + jnp.log(denominator)
        probability = jnp.where(allowed, jnp.exp(product - log_total), 0.0)
        grad_probs = jnp.einsum(
            "gqf,gnkf->gqnk", grad_head, value_tile, preferred_element_type=jnp.float32
        )
        row_delta = jnp.sum(probability * grad_probs, axis=(2, 3), keepdims=True)
        grad_scores = (probability * (grad_probs - row_delta)).astype(jnp.bfloat16)
        prob_low = probability.astype(jnp.bfloat16)
        query_term = (
            jnp.einsum("gqnk,gnkf->gqf", grad_scores, key_tile, preferred_element_type=jnp.float32)
            * score_scale
        )
        query_sum = query_sum + jnp.where(column_mask, query_term, 0.0)
        key_sum = (
            key_sum
            + jnp.einsum(
                "gqnk,gqf->gnkf", grad_scores, query_head, preferred_element_type=jnp.float32
            )
            * score_scale
        )
        value_sum = value_sum + jnp.einsum(
            "gqnk,gqf->gnkf", prob_low, grad_head, preferred_element_type=jnp.float32
        )
        logs.append(log_total[:, :, 0, 0])
        deltas.append(row_delta[:, :, 0, 0])
    return (query_sum, key_sum, value_sum, jnp.stack(logs, axis=1), jnp.stack(deltas, axis=1))


def per_device(queries, keys_in, values, d_out, token_count, block_ids, neighbours):
    head_count = lax.axis_size("head")
    blk_count = lax.axis_size("blk")
    blk_index = lax.axis_index("blk")
    shard_rows = queries.shape[0]
    block_rows = BLK
    head_width = HD
    score_scale = 1.0 / math.sqrt(head_width)
    query_rows, key_rows, value_rows, grad_rows = (
        lax.all_to_all(queries, "head", split_axis=1, concat_axis=0, tiled=True),
        lax.all_to_all(keys_in, "head", split_axis=1, concat_axis=0, tiled=True),
        lax.all_to_all(values, "head", split_axis=1, concat_axis=0, tiled=True),
        lax.all_to_all(d_out, "head", split_axis=1, concat_axis=0, tiled=True),
    )
    feature_width = query_rows.shape[1]
    masks = head_masks(feature_width, head_width)
    local_blocks = query_rows.shape[0] // block_rows
    key_slots, query_where, key_where = block_tables(
        block_ids, neighbours, blk_count, head_count, block_rows, shard_rows
    )
    token_limit = token_count[0]
    first_slot = blk_index * local_blocks
    my_key_slots = lax.dynamic_slice_in_dim(key_slots, first_slot, local_blocks, 0)
    my_query_where = lax.dynamic_slice_in_dim(query_where, first_slot, local_blocks, 0)
    my_key_where = lax.dynamic_slice_in_dim(key_where, first_slot, local_blocks, 0)
    row_valid = (my_query_where < token_limit).reshape(-1, 1)
    grad_rows = jnp.where(row_valid, grad_rows, jnp.zeros_like(grad_rows))
    query_blocks = query_rows.reshape(local_blocks, block_rows, feature_width)
    grad_blocks = grad_rows.reshape(local_blocks, block_rows, feature_width)
    gathered_keys, gathered_values = (
        lax.all_gather(key_rows, "blk", axis=0, tiled=True),
        lax.all_gather(value_rows, "blk", axis=0, tiled=True),
    )
    key_blocks = gathered_keys.reshape(-1, block_rows, feature_width)
    value_blocks = gathered_values.reshape(-1, block_rows, feature_width)
    group_blocks = group_size(local_blocks, block_rows)
    steps_count = local_blocks // group_blocks

    def local_tiles(start_block):
        query_tile = lax.dynamic_slice_in_dim(query_blocks, start_block, group_blocks, 0)
        grad_tile = lax.dynamic_slice_in_dim(grad_blocks, start_block, group_blocks, 0)
        slot_tile = lax.dynamic_slice_in_dim(my_key_slots, start_block, group_blocks, 0)
        key_tile = jnp.take(key_blocks, slot_tile, axis=0)
        value_tile = jnp.take(value_blocks, slot_tile, axis=0)
        allowed = permitted(
            lax.dynamic_slice_in_dim(my_query_where, start_block, group_blocks, 0),
            lax.dynamic_slice_in_dim(my_key_where, start_block, group_blocks, 0),
            token_limit,
        )
        return (query_tile, grad_tile, slot_tile, key_tile, value_tile, allowed)

    def summed_step(running, step_index):
        query_tile, grad_tile, slot_tile, key_tile, value_tile, allowed = local_tiles(
            step_index * group_blocks
        )
        query_part, key_part, value_part, log_total, row_delta = attend_all(
            query_tile, key_tile, value_tile, grad_tile, allowed, masks, score_scale
        )
        flat_slots = slot_tile.reshape(-1)
        key_sum = running[0].at[flat_slots].add(key_part.reshape(-1, block_rows, feature_width))
        value_sum = running[1].at[flat_slots].add(value_part.reshape(-1, block_rows, feature_width))
        return ((key_sum, value_sum), query_part)

    zero_acc = jnp.zeros((key_blocks.shape[0], block_rows, feature_width), jnp.float32)
    (key_sum, value_sum), query_parts = lax.scan(
        summed_step, (zero_acc, zero_acc), jnp.arange(steps_count, dtype=jnp.int32)
    )
    key_mine, value_mine = (
        lax.psum_scatter(
            key_sum.astype(jnp.bfloat16), "blk", scatter_dimension=0, tiled=True
        ).astype(jnp.float32),
        lax.psum_scatter(
            value_sum.astype(jnp.bfloat16), "blk", scatter_dimension=0, tiled=True
        ).astype(jnp.float32),
    )
    query_grad_rows = query_parts.reshape(local_blocks * block_rows, feature_width).astype(
        jnp.bfloat16
    )
    key_grad_rows = key_mine.reshape(local_blocks * block_rows, feature_width).astype(jnp.bfloat16)
    value_grad_rows = value_mine.reshape(local_blocks * block_rows, feature_width).astype(
        jnp.bfloat16
    )
    gradients = (
        lax.all_to_all(query_grad_rows, "head", split_axis=0, concat_axis=1, tiled=True),
        lax.all_to_all(key_grad_rows, "head", split_axis=0, concat_axis=1, tiled=True),
        lax.all_to_all(value_grad_rows, "head", split_axis=0, concat_axis=1, tiled=True),
    )
    return (gradients[0], gradients[1], gradients[2])


def solution(mesh):
    return jax.shard_map(
        per_device,
        mesh=mesh,
        in_specs=(
            P(("bend", "head", "blk"), None),
            P(("bend", "head", "blk"), None),
            P(("bend", "head", "blk"), None),
            P(("bend", "head", "blk"), None),
            P("bend"),
            P("bend"),
            P("bend", None),
        ),
        out_specs=(
            P(("bend", "head", "blk"), None),
            P(("bend", "head", "blk"), None),
            P(("bend", "head", "blk"), None),
        ),
        check_vma=False,
    )
```

profile of v0, /device:TPU:0, one launch (start us, length us, event | category | flops | bytes accessed | tf_op | source)
XLA Modules:
  0.0 177.6 jit_solution(13463688211217680719)
XLA Ops:
  7.2 1.8 %copy.45 = bf16[128,1024]{0,1:T(8,128)(2,1)} copy(bf16[128,1024]{1,0:T(8,128)(2,1)} %param.10) | data formatting | bytes 524288 | tf_op args[1]
  9.0 6.3 %all-to-all-start.1 = ((bf16[128,4,256]{0,2,1:T(8,128)(2,1)}), bf16[128,4,256]{0,2,1:T(8,128)(2,1)S(1)}, u32[]{:S(2)}, u32[]{:S(2)}) async-start(bf16[128,4,256]{0,2,1:T(8,128)(2,1)} %bitcast.4), calls=%async_computation.1 | async-start | bytes 524288 | tf_op jit(solution)/shard_map/all_to_all | solution.py:120
  15.4 0.8 select_reduce_fusion.11
  16.4 0.8 copy.41
  17.2 0.2 select_reduce_fusion.9
  17.4 0.3 select_reduce_fusion.8
  17.9 1.8 %copy.51 = bf16[128,1024]{0,1:T(8,128)(2,1)} copy(bf16[128,1024]{1,0:T(8,128)(2,1)} %param.11) | data formatting | bytes 524288 | tf_op args[2]
  19.7 4.5 %all-to-all-done.1 = bf16[128,4,256]{0,2,1:T(8,128)(2,1)S(1)} async-done(((bf16[128,4,256]{0,2,1:T(8,128)(2,1)}), bf16[128,4,256]{0,2,1:T(8,128)(2,1)S(1)}, u32[]{:S(2)}, u32[]{:S(2)}) %all-to-all-start.1) | async-done | bytes 262176 | tf_op jit(solution)/shard_map/all_to_all | solution.py:120
  24.3 3.4 %all-to-all-start.3 = ((bf16[128,4,256]{0,2,1:T(8,128)(2,1)}), bf16[128,4,256]{0,2,1:T(8,128)(2,1)S(1)}, u32[]{:S(2)}, u32[]{:S(2)}) async-start(bf16[128,4,256]{0,2,1:T(8,128)(2,1)} %bitcast.13), calls=%async_computation.3 | async-start | bytes 524288 | tf_op jit(solution)/shard_map/all_to_all | solution.py:121
  27.7 0.9 copy.46
  28.9 0.7 copy.83
  30.7 4.0 %all-to-all-done.3 = bf16[128,4,256]{0,2,1:T(8,128)(2,1)S(1)} async-done(((bf16[128,4,256]{0,2,1:T(8,128)(2,1)}), bf16[128,4,256]{0,2,1:T(8,128)(2,1)S(1)}, u32[]{:S(2)}, u32[]{:S(2)}) %all-to-all-start.3) | async-done | bytes 262176 | tf_op jit(solution)/shard_map/all_to_all | solution.py:121
  34.7 3.4 %all-to-all-start = ((bf16[128,4,256]{2,0,1:T(8,128)(2,1)}), bf16[128,4,256]{2,0,1:T(8,128)(2,1)S(1)}, u32[]{:S(2)}, u32[]{:S(2)}) async-start(bf16[128,4,256]{2,0,1:T(8,128)(2,1)} %bitcast.165), calls=%async_computation | async-start | bytes 524288 | tf_op jit(solution)/shard_map/all_to_all | solution.py:119
  38.4 0.9 copy.49
  39.4 0.9 copy.52
  40.3 18.7 %all-gather.3.cloned.1.call-done = bf16[2048,256]{1,0:T(8,128)(2,1)} async-done(((bf16[512,256]{1,0:T(8,128)(2,1)}), bf16[2048,256]{1,0:T(8,128)(2,1)}) %all-gather.3.cloned.1.call-update) | async-done | bytes 1048592 | tf_op jit(solution)/shard_map/all_gather | solution.py:140
  59.0 1.9 %gather_fusion = bf16[40,128,256]{2,1,0:T(8,128)(2,1)S(1)} fusion(bf16[16,128,256]{2,1,0:T(8,128)(2,1)} %bitcast.179, s32[1024]{0:T(1024)S(1)} %pad_clamp_fusion), kind=kCustom, calls=%fused_computation.clone | custom fusion | bytes 5243040 | tf_op jit(solution)/shard_map/while/body/eval_jaxpr/jit(_take)/gather | solution.py:152
  61.0 4.6 %all-to-all-start.2 = ((bf16[128,4,256]{2,0,1:T(8,128)(2,1)}), bf16[128,4,256]{2,0,1:T(8,128)(2,1)S(1)}, u32[]{:S(2)}, u32[]{:S(2)}) async-start(bf16[128,4,256]{2,0,1:T(8,128)(2,1)} %copy.49), calls=%async_computation.2 | async-start | bytes 524288 | tf_op jit(solution)/shard_map/all_to_all | solution.py:122
  65.6 0.9 fusion.28
  66.5 0.9 fusion.29
  67.4 0.9 fusion.30
  68.4 2.2 %select_reduce_fusion.1 = (f32[4,128]{1,0:T(4,128)S(1)}, f32[4,128]{1,0:T(4,128)S(1)}, f32[4,128]{1,0:T(4,128)S(1)}, f32[4,128]{1,0:T(4,128)S(1)}, f32[4,128,10,128]{1,3,2,0:T(8,128)S(1)}) fusion(s32[4,128]{1,0:T(4,128)S(1)} %iota_add_fusion.1, s32[4,10,128]{2,1,0:T(8,128)S(1)} %iota_add_fusion, pred[4,10,128]{2,1,0:T(8,128)(4,1)S(1)} %broadcast_compare_fusion, ...), kind=kOutput, calls=%fused_computation.10 | convolution fusion | flops 346159104 | bytes 13405480 | tf_op jit(solution)/shard_map/while/body/eval_jaxpr/gqf,gnkf->gqnk/dot_general | solution.py:75
  70.6 2.9 %select_reduce_fusion = (f32[4,128]{1,0:T(4,128)S(1)}, f32[4,128]{1,0:T(4,128)S(1)}, f32[4,128]{1,0:T(4,128)S(1)}, f32[4,128]{1,0:T(4,128)S(1)}) fusion(f32[4,128,10,128]{1,3,2,0:T(8,128)S(1)} %get-tuple-element.74, f32[4,128]{1,0:T(4,128)S(1)} %get-tuple-element.60, s32[4,128]{1,0:T(4,128)S(1)} %iota_add_fusion.1, s32[4,10,128]{2,1,0:T(8,128)S(1)} %iota_add_fusion, ...), kind=kLoop, calls=%fused_computation.9 | loop fusion | flops 11794432 | bytes 10529792 | tf_op jit(solution)/shard_map/while/body/eval_jaxpr/reduce_sum | solution.py:79
  73.5 1.0 all-to-all-done.2
  74.5 4.0 %fusion.11 = f32[4,10,128,256]{3,2,1,0:T(8,128)S(1)} fusion(f32[4,128,10,128]{1,3,2,0:T(8,128)} %copy-done.5, f32[4,128]{1,0:T(4,128)S(1)} %get-tuple-element.78, s32[4,128]{1,0:T(4,128)S(1)} %iota_add_fusion.1, s32[4,10,128]{2,1,0:T(8,128)S(1)} %iota_add_fusion, pred[4,10,128]{2,1,0:T(8,128)(4,1)S(1)} %broadcast_compare_fusion, ...), kind=kOutput, calls=%fused_computation.40 | convolution fusion | flops 339738624 | bytes 8156928 | tf_op jit(solution)/shard_map/while/body/eval_jaxpr/gqnk,gqf->gnkf/dot_general | solution.py:102
  78.6 1.6 fusion.13
  80.4 1.6 fusion.9
  82.2 3.8 %add_add_fusion = f32[4,10,128,256]{3,2,1,0:T(8,128)} fusion(f32[4,10,128,256]{3,2,1,0:T(8,128)S(1)} %fusion.9, f32[4,10,128,256]{3,2,1,0:T(8,128)S(1)} %fusion.13, f32[4,10,128,256]{3,2,1,0:T(8,128)S(1)} %fusion.11, f32[4,128,10,128]{1,3,2,0:T(8,128)S(1)} %copy-done.11, f32[4,128]{1,0:T(4,128)S(1)} %get-tuple-element.76, s32[4,128]{1,0:T(4,128)S(1)} %iota_add_fusion.1, ...), kind=kOutput, calls=%fused_computation.4 | convolution fusion | flops 343670784 | bytes 23885568 | tf_op jit(solution)/shard_map/while/body/eval_jaxpr/gqnk,gqf->gnkf/dot_general | solution.py:102
  86.0 0.2 broadcast_in_dim.201.clone.1
  86.2 9.1 %scatter_fusion.1 = f32[16,128,256]{2,1,0:T(8,128)S(1)} fusion(f32[16,128,256]{2,1,0:T(8,128)S(1)} %broadcast_in_dim.201.clone.1, s32[40]{0:T(128)S(1)} %fusion.68, f32[40,128,256]{2,1,0:T(8,128)} %bitcast.177), kind=kCustom, calls=%fused_computation.3 | custom fusion | flops 1310720 | bytes 15728800 | tf_op jit(solution)/shard_map/while/body/eval_jaxpr/scatter-add | solution.py:170
  95.3 1.1 convert_element_type.58
  96.4 0.3 reduce-scatter.3.cloned.1.call-start
  96.7 1.9 %gather_fusion.1 = bf16[40,128,256]{2,1,0:T(8,128)(2,1)S(1)} fusion(bf16[16,128,256]{2,1,0:T(8,128)(2,1)} %bitcast.178, s32[1024]{0:T(1024)S(1)} %pad_clamp_fusion), kind=kCustom, calls=%fused_computation.1.clone | custom fusion | bytes 5243040 | tf_op jit(solution)/shard_map/while/body/eval_jaxpr/jit(_take)/gather | solution.py:153
  98.6 0.9 fusion.1
  99.6 0.9 fusion.2
  100.6 0.9 fusion.3
  101.5 0.6 copy-done.12
  102.1 1.1 copy-done.4
  103.2 0.8 copy-done.6
  104.1 3.8 %multiply_reduce_fusion = (f32[4,128]{1,0:T(4,128)S(1)}, f32[4,128]{1,0:T(4,128)S(1)}, f32[4,128]{1,0:T(4,128)S(1)}, f32[4,128]{1,0:T(4,128)S(1)}, f32[4,128,10,128]{1,3,2,0:T(8,128)S(1)}) fusion(f32[4,128]{1,0:T(4,128)S(1)} %get-tuple-element.76, f32[4,128,10,128]{1,3,2,0:T(8,128)S(1)} %copy-done.12, s32[4,128]{1,0:T(4,128)S(1)} %iota_add_fusion.1, ...), kind=kOutput, calls=%fused_computation.7 | convolution fusion | flops 351533056 | bytes 23899944 | tf_op jit(solution)/shard_map/while/body/eval_jaxpr/gqf,gnkf->gqnk/dot_general | solution.py:84
  107.9 4.2 %multiply_convert_fusion = (bf16[4,128,10,128]{1,3,2,0:T(8,128)(2,1)S(1)}, bf16[4,128,10,128]{1,3,2,0:T(8,128)(2,1)S(1)}, bf16[4,128,10,128]{1,3,2,0:T(8,128)(2,1)S(1)}, bf16[4,128,10,128]{1,3,2,0:T(8,128)(2,1)S(1)}) fusion(f32[4,128,10,128]{1,3,2,0:T(8,128)S(1)} %get-tuple-element.75, f32[4,128]{1,0:T(4,128)S(1)} %get-tuple-element.52, ...), kind=kLoop, calls=%fused_computation.6 | loop fusion | flops 17039360 | bytes 26258432 | tf_op jit(solution)/shard_map/while/body/eval_jaxpr/convert_element_type | solution.py:88
  112.1 0.8 fusion.41
  113.0 0.3 copy-done.13
  113.3 0.3 copy-done.15
  113.6 0.8 fusion.44
  114.4 0.8 fusion.47
  115.3 3.3 %add_multiply_fusion = f32[4,10,128,256]{3,2,1,0:T(8,128)} fusion(f32[4,10,128,256]{3,2,1,0:T(8,128)S(1)} %fusion.41, f32[4,10,128,256]{3,2,1,0:T(8,128)S(1)} %fusion.47, f32[4,10,128,256]{3,2,1,0:T(8,128)S(1)} %fusion.44, bf16[4,128,10,128]{1,3,2,0:T(8,128)(2,1)S(1)} %get-tuple-element.70, bf16[128,4,256]{2,0,1:T(8,128)(2,1)S(1)} %all-to-all-done, ...), kind=kOutput, calls=%fused_computation.5 | convolution fusion | flops 340918272 | bytes 22544640 | tf_op jit(solution)/shard_map/while/body/eval_jaxpr/gqnk,gqf->gnkf/dot_general | solution.py:97
  118.8 9.1 %scatter_fusion = f32[16,128,256]{2,1,0:T(8,128)S(1)} fusion(f32[16,128,256]{2,1,0:T(8,128)S(1)} %broadcast_in_dim.201.clone, s32[40]{0:T(128)S(1)} %fusion.68, f32[40,128,256]{2,1,0:T(8,128)} %bitcast.176), kind=kCustom, calls=%fused_computation.2 | custom fusion | flops 1310720 | bytes 15728800 | tf_op jit(solution)/shard_map/while/body/eval_jaxpr/scatter-add | solution.py:169
  127.9 1.1 convert_element_type.53
  129.1 3.0 %fusion.20 = f32[4,128,256]{2,1,0:T(8,128)S(1)} fusion(bf16[4,128,10,128]{1,3,2,0:T(8,128)(2,1)} %copy-done.15, bf16[4,10,128,256]{3,2,1,0:T(8,128)(2,1)} %bitcast.172, pred[4,10]{1,0:T(4,128)(4,1)S(1)} %copy.44, pred[256]{0:T(512)(128)(4,1)S(1)} %get-tuple-element.66), kind=kOutput, calls=%fused_computation.52 | convolution fusion | flops 337117184 | bytes 4456744 | tf_op jit(solution)/shard_map/while/body/eval_jaxpr/gqnk,gnkf->gqf/dot_general | solution.py:91
  132.1 0.3 copy-done.14
  132.3 0.8 fusion.18
  133.1 0.8 fusion.24
  133.9 0.5 copy-done.17
  134.4 0.8 fusion.26
  135.2 12.1 %all_to_all.115 = bf16[4,128,256]{2,1,0:T(8,128)(2,1)S(1)} all-to-all(bf16[4,128,256]{2,1,0:T(8,128)(2,1)S(1)} %fusion.26), channel_id=1, replica_groups=mesh['bend'=2,'head'=4,'blk'=4] {'head'}, dimensions={0} | all-to-all | bytes 524288 | tf_op jit(solution)/shard_map/all_to_all | solution.py:193
  147.3 3.4 %all-to-all-start.6 = ((bf16[4,128,256]{2,1,0:T(8,128)(2,1)}), bf16[4,128,256]{2,1,0:T(8,128)(2,1)S(1)}, u32[]{:S(2)}, u32[]{:S(2)}) async-start(bf16[4,128,256]{2,1,0:T(8,128)(2,1)} %reduce-scatter.5.cloned.1.call-done), calls=%async_computation.8 | async-start | bytes 524288 | tf_op jit(solution)/shard_map/all_to_all | solution.py:195
  150.7 5.6 %reduce-scatter.3.cloned.1.call-done = bf16[4,128,256]{2,1,0:T(8,128)(2,1)} async-done(((bf16[16,128,256]{2,1,0:T(8,128)(2,1)}), bf16[4,128,256]{2,1,0:T(8,128)(2,1)}) %reduce-scatter.3.cloned.1.call-update) | async-done | bytes 262160 | tf_op jit(solution)/shard_map/reduce_scatter | solution.py:178
  156.4 2.3 %all-to-all-done.6 = bf16[4,128,256]{2,1,0:T(8,128)(2,1)S(1)} async-done(((bf16[4,128,256]{2,1,0:T(8,128)(2,1)}), bf16[4,128,256]{2,1,0:T(8,128)(2,1)S(1)}, u32[]{:S(2)}, u32[]{:S(2)}) %all-to-all-start.6) | async-done | bytes 262176 | tf_op jit(solution)/shard_map/all_to_all | solution.py:195
  158.7 3.4 %all-to-all-start.5 = ((bf16[4,128,256]{2,1,0:T(8,128)(2,1)}), bf16[4,128,256]{2,1,0:T(8,128)(2,1)S(1)}, u32[]{:S(2)}, u32[]{:S(2)}) async-start(bf16[4,128,256]{2,1,0:T(8,128)(2,1)} %reduce-scatter.3.cloned.1.call-done), calls=%async_computation.6 | async-start | bytes 524288 | tf_op jit(solution)/shard_map/all_to_all | solution.py:194
  162.2 0.9 copy.62
  163.3 0.9 copy.64
  164.1 5.9 %all-to-all-done.5 = bf16[4,128,256]{2,1,0:T(8,128)(2,1)S(1)} async-done(((bf16[4,128,256]{2,1,0:T(8,128)(2,1)}), bf16[4,128,256]{2,1,0:T(8,128)(2,1)S(1)}, u32[]{:S(2)}, u32[]{:S(2)}) %all-to-all-start.5) | async-done | bytes 262176 | tf_op jit(solution)/shard_map/all_to_all | solution.py:194
  170.2 0.9 copy.63
  (74 shorter events, 2.7 us)
Async XLA Ops:
  7.2 21.7 %copy-start.18 = (bf16[128,1024]{1,0:T(8,128)(2,1)S(1)}, bf16[128,1024]{1,0:T(8,128)(2,1)}, u32[]{:S(2)}) copy-start(bf16[128,1024]{1,0:T(8,128)(2,1)} %param.9) | copy-start | bytes 786436
  7.2 31.1 %copy-start.19 = (bf16[128,1024]{1,0:T(8,128)(2,1)S(1)}, bf16[128,1024]{1,0:T(8,128)(2,1)}, u32[]{:S(2)}) copy-start(bf16[128,1024]{1,0:T(8,128)(2,1)} %param.12) | copy-start | bytes 786436
  9.0 15.2 %all-to-all-start.1 = ((bf16[128,4,256]{0,2,1:T(8,128)(2,1)}), bf16[128,4,256]{0,2,1:T(8,128)(2,1)S(1)}, u32[]{:S(2)}, u32[]{:S(2)}) async-start(bf16[128,4,256]{0,2,1:T(8,128)(2,1)} %bitcast.4), calls=%async_computation.1 | async-start | bytes 524288 | tf_op jit(solution)/shard_map/all_to_all | solution.py:120
  24.3 10.4 %all-to-all-start.3 = ((bf16[128,4,256]{0,2,1:T(8,128)(2,1)}), bf16[128,4,256]{0,2,1:T(8,128)(2,1)S(1)}, u32[]{:S(2)}, u32[]{:S(2)}) async-start(bf16[128,4,256]{0,2,1:T(8,128)(2,1)} %bitcast.13), calls=%async_computation.3 | async-start | bytes 524288 | tf_op jit(solution)/shard_map/all_to_all | solution.py:121
  27.7 31.3 %all-gather.3.cloned.1.call-start = ((), (), s32[]{:S(2)}) async-start(), calls=%async_computation.9 | async-start | bytes 1310720 | tf_op jit(solution)/shard_map/all_gather | solution.py:140
  34.7 26.3 %all-to-all-start = ((bf16[128,4,256]{2,0,1:T(8,128)(2,1)}), bf16[128,4,256]{2,0,1:T(8,128)(2,1)S(1)}, u32[]{:S(2)}, u32[]{:S(2)}) async-start(bf16[128,4,256]{2,0,1:T(8,128)(2,1)} %bitcast.165), calls=%async_computation | async-start | bytes 524288 | tf_op jit(solution)/shard_map/all_to_all | solution.py:119
  38.1 58.6 %all-gather.5.cloned.1.call-start = ((), (), s32[]{:S(2)}) async-start(), calls=%async_computation.10 | async-start | bytes 1310720 | tf_op jit(solution)/shard_map/all_gather | solution.py:141
  61.0 7.4 %copy-start = (bf16[40,128,256]{2,1,0:T(8,128)(2,1)}, bf16[40,128,256]{2,1,0:T(8,128)(2,1)S(1)}, u32[]{:S(2)}) copy-start(bf16[40,128,256]{2,1,0:T(8,128)(2,1)S(1)} %gather_fusion) | copy-start | bytes 7864324
  61.0 13.5 %all-to-all-start.2 = ((bf16[128,4,256]{2,0,1:T(8,128)(2,1)}), bf16[128,4,256]{2,0,1:T(8,128)(2,1)S(1)}, u32[]{:S(2)}, u32[]{:S(2)}) async-start(bf16[128,4,256]{2,0,1:T(8,128)(2,1)} %copy.49), calls=%async_computation.2 | async-start | bytes 524288 | tf_op jit(solution)/shard_map/all_to_all | solution.py:122
  65.6 81.7 %reduce-scatter.5.cloned.1.call-start = ((), (), s32[]{:S(2)}) async-start(), calls=%async_computation.12 | async-start | bytes 1310720 | tf_op jit(solution)/shard_map/reduce_scatter | solution.py:181
  66.5 4.1 %copy-start.2 = (f32[4,128,10,128]{1,3,2,0:T(8,128)}, f32[4,128,10,128]{1,3,2,0:T(8,128)S(1)}, u32[]{:S(2)}) copy-start(f32[4,128,10,128]{1,3,2,0:T(8,128)S(1)} %fusion.28) | copy-start | bytes 7864324
  67.4 3.2 %copy-start.5 = (f32[4,128,10,128]{1,3,2,0:T(8,128)}, f32[4,128,10,128]{1,3,2,0:T(8,128)S(1)}, u32[]{:S(2)}) copy-start(f32[4,128,10,128]{1,3,2,0:T(8,128)S(1)} %fusion.29) | copy-start | bytes 7864324
  68.3 2.3 %copy-start.7 = (f32[4,128,10,128]{1,3,2,0:T(8,128)}, f32[4,128,10,128]{1,3,2,0:T(8,128)S(1)}, u32[]{:S(2)}) copy-start(f32[4,128,10,128]{1,3,2,0:T(8,128)S(1)} %fusion.30) | copy-start | bytes 7864324
  70.6 2.9 %copy-start.10 = (f32[4,128,10,128]{1,3,2,0:T(8,128)}, f32[4,128,10,128]{1,3,2,0:T(8,128)S(1)}, u32[]{:S(2)}) copy-start(f32[4,128,10,128]{1,3,2,0:T(8,128)S(1)} %get-tuple-element.74) | copy-start | bytes 7864324
  74.5 4.1 %copy-start.8 = (f32[4,128,10,128]{1,3,2,0:T(8,128)S(1)}, f32[4,128,10,128]{1,3,2,0:T(8,128)}, u32[]{:S(2)}) copy-start(f32[4,128,10,128]{1,3,2,0:T(8,128)} %copy-done.7) | copy-start | bytes 7864324
  78.6 1.8 %copy-start.3 = (f32[4,128,10,128]{1,3,2,0:T(8,128)S(1)}, f32[4,128,10,128]{1,3,2,0:T(8,128)}, u32[]{:S(2)}) copy-start(f32[4,128,10,128]{1,3,2,0:T(8,128)} %copy-done.2) | copy-start | bytes 7864324
  80.4 1.7 copy-start.11
  96.4 60.0 %reduce-scatter.3.cloned.1.call-start = ((), (), s32[]{:S(2)}) async-start(), calls=%async_computation.11 | async-start | bytes 1310720 | tf_op jit(solution)/shard_map/reduce_scatter | solution.py:178
  99.6 1.9 %copy-start.9 = (f32[4,128,10,128]{1,3,2,0:T(8,128)S(1)}, f32[4,128,10,128]{1,3,2,0:T(8,128)}, u32[]{:S(2)}) copy-start(f32[4,128,10,128]{1,3,2,0:T(8,128)} %copy-done.7) | copy-start | bytes 7864324
  99.6 2.5 %copy-start.12 = (f32[4,128,10,128]{1,3,2,0:T(8,128)S(1)}, f32[4,128,10,128]{1,3,2,0:T(8,128)}, u32[]{:S(2)}) copy-start(f32[4,128,10,128]{1,3,2,0:T(8,128)} %copy-done.10) | copy-start | bytes 7864324
  100.5 2.7 %copy-start.4 = (f32[4,128,10,128]{1,3,2,0:T(8,128)S(1)}, f32[4,128,10,128]{1,3,2,0:T(8,128)}, u32[]{:S(2)}) copy-start(f32[4,128,10,128]{1,3,2,0:T(8,128)} %copy-done.2) | copy-start | bytes 7864324
  100.5 3.5 %copy-start.6 = (f32[4,128,10,128]{1,3,2,0:T(8,128)S(1)}, f32[4,128,10,128]{1,3,2,0:T(8,128)}, u32[]{:S(2)}) copy-start(f32[4,128,10,128]{1,3,2,0:T(8,128)} %copy-done.5) | copy-start | bytes 7864324
  112.1 1.2 copy-start.13
  112.1 1.5 copy-start.15
  112.1 3.2 %copy-start.16 = (bf16[4,128,10,128]{1,3,2,0:T(8,128)(2,1)}, bf16[4,128,10,128]{1,3,2,0:T(8,128)(2,1)S(1)}, u32[]{:S(2)}) copy-start(bf16[4,128,10,128]{1,3,2,0:T(8,128)(2,1)S(1)} %get-tuple-element.70) | copy-start | bytes 3932164
  129.0 3.0 %copy-start.1 = (bf16[40,128,256]{2,1,0:T(8,128)(2,1)S(1)}, bf16[40,128,256]{2,1,0:T(8,128)(2,1)}, u32[]{:S(2)}) copy-start(bf16[40,128,256]{2,1,0:T(8,128)(2,1)} %copy-done) | copy-start | bytes 7864324
  129.0 3.3 %copy-start.14 = (bf16[4,128,10,128]{1,3,2,0:T(8,128)(2,1)S(1)}, bf16[4,128,10,128]{1,3,2,0:T(8,128)(2,1)}, u32[]{:S(2)}) copy-start(bf16[4,128,10,128]{1,3,2,0:T(8,128)(2,1)} %copy-done.13) | copy-start | bytes 3932164
  133.1 1.3 copy-start.17
  147.3 11.3 %all-to-all-start.6 = ((bf16[4,128,256]{2,1,0:T(8,128)(2,1)}), bf16[4,128,256]{2,1,0:T(8,128)(2,1)S(1)}, u32[]{:S(2)}, u32[]{:S(2)}) async-start(bf16[4,128,256]{2,1,0:T(8,128)(2,1)} %reduce-scatter.5.cloned.1.call-done), calls=%async_computation.8 | async-start | bytes 524288 | tf_op jit(solution)/shard_map/all_to_all | solution.py:195
  158.7 11.4 %all-to-all-start.5 = ((bf16[4,128,256]{2,1,0:T(8,128)(2,1)}), bf16[4,128,256]{2,1,0:T(8,128)(2,1)S(1)}, u32[]{:S(2)}, u32[]{:S(2)}) async-start(bf16[4,128,256]{2,1,0:T(8,128)(2,1)} %reduce-scatter.3.cloned.1.call-done), calls=%async_computation.6 | async-start | bytes 524288 | tf_op jit(solution)/shard_map/all_to_all | solution.py:194
Sparse Core Ops, SparseCore 0:
  30.9 28.0 all-gather.2
  61.4 26.6 all-gather.4
  96.5 27.2 reduce-scatter.4
  129.2 27.1 reduce-scatter.2
where the time goes:
time: 179 us; the launch traced here: 178 us
  waiting for transfers between devices  42.2 us (24%)
  matrix products  33.8 us (19%)
  other arithmetic  29.5 us (16%)
  starting transfers between devices  24.9 us (14%)
  local copies, waits for them, and re-layouts  20.2 us (11%)
  between operations  14.9 us (8%)
  blocking collectives  12.1 us (7%)
    all_gather x1, waiting for transfers between devices, per_device(): lax.all_gather(key_rows, 'blk', axis=0, tiled=True)  18.7 us
    all_to_all x1, blocking collectives, per_device(): lax.all_to_all(query_grad_rows, 'head', split_axis=0, concat_axis=1, tile...  12.1 us
    unnamed x47, local copies, waits for them, and re-layouts  11.5 us
    dot_general x4, matrix products, attend_all(): jnp.einsum('gqnk,gqf->gnkf', prob_low, grad_head, preferred_element_type=...  11.1 us
    scatter-add x1, other arithmetic, summed_step(): running[0].at[flat_slots]  9.11 us
    scatter-add x1, other arithmetic, summed_step(): running[1].at[flat_slots]  9.09 us
    dot_general x4, matrix products, attend_all(): jnp.einsum('gqf,gnkf->gqnk', grad_head, value_tile, preferred_element_typ...  6.59 us
    all_to_all x1, starting transfers between devices, per_device(): lax.all_to_all(keys_in, 'head', split_axis=1, concat_axis=0, tiled=True)  6.32 us
  transfers between devices with their start and end apart: 10, of which 7 were waited for; matrix products, arithmetic and copies ran while one was open for 43% of the time, Pallas kernels for 0%

commit v1 on v0

--- a/solution.py
+++ b/solution.py
@@ -1,8 +1,11 @@
+import functools
 import math
 
 import jax
 import jax.numpy as jnp
 from jax import lax
+from jax.experimental import pallas as pl
+from jax.experimental.pallas import tpu as pltpu
 from jax.sharding import PartitionSpec as P
 
 HD = 64
@@ -197,9 +200,321 @@
     return (gradients[0], gradients[1], gradients[2])
 
 
+def head_kernel(
+    ring,
+    blk_count,
+    near,
+    limit_ref,
+    ids_ref,
+    nbr_ref,
+    q_ref,
+    k_ref,
+    v_ref,
+    g_ref,
+    gq_out,
+    gk_out,
+    gv_out,
+    qk_send,
+    gv_send,
+    qk_land,
+    gv_land,
+    kt_buf,
+    work,
+    prob_wide,
+    prob_low,
+    dscores,
+    out_send,
+    out_land,
+    stored_of,
+    slot_of,
+    term_at,
+    send_sem,
+    recv_sem,
+):
+    rows = BLK
+    width = HD
+    scale = 1.0 / math.sqrt(width)
+    me = lax.axis_index("head") * blk_count + lax.axis_index("blk")
+    limit = limit_ref[0]
+
+    def place(peer):
+        return {"head": lax.div(peer, blk_count), "blk": lax.rem(peer, blk_count)}
+
+    def copy_to(kind, source, target, slot, peer):
+        return pltpu.make_async_remote_copy(
+            src_ref=source,
+            dst_ref=target,
+            send_sem=send_sem.at[kind, slot],
+            recv_sem=recv_sem.at[kind, me],
+            device_id=place(peer),
+            device_id_type=pl.DeviceIdType.MESH,
+        )
+
+    def await_from(kind, target, peer):
+        pltpu.make_async_remote_copy(
+            src_ref=target,
+            dst_ref=target,
+            send_sem=send_sem.at[kind, peer],
+            recv_sem=recv_sem.at[kind, peer],
+            device_id=place(peer),
+            device_id_type=pl.DeviceIdType.MESH,
+        ).wait_recv()
+
+    def others(body):
+        def step(distance, carry):
+            body(lax.rem(me + distance, ring))
+            return carry
+
+        lax.fori_loop(1, ring, step, 0)
+
+    barrier = pltpu.get_barrier_semaphore()
+    others(
+        lambda peer: pl.semaphore_signal(
+            barrier, inc=1, device_id=place(peer), device_id_type=pl.DeviceIdType.MESH
+        )
+    )
+
+    row_index = lax.broadcasted_iota(jnp.int32, (rows, 2 * width), 0)
+
+    my_limit = limit - ids_ref[me] * rows
+    for pair in range(ring // 2):
+        columns = slice(pair * 2 * width, (pair + 1) * 2 * width)
+        q_tile = q_ref[:, columns] * jnp.asarray(scale, jnp.bfloat16)
+        k_tile = k_ref[:, columns]
+        g_tile = jnp.where(row_index < my_limit, g_ref[:, columns].astype(jnp.float32), 0.0)
+        g_tile = g_tile.astype(jnp.bfloat16)
+        v_tile = v_ref[:, columns]
+        for side in range(2):
+            part = slice(side * width, (side + 1) * width)
+            qk_send[2 * pair + side] = jnp.concatenate([q_tile[:, part], k_tile[:, part]], axis=1)
+            gv_send[2 * pair + side] = jnp.concatenate([g_tile[:, part], v_tile[:, part]], axis=1)
+
+    pl.semaphore_wait(barrier, ring - 1)
+    others(lambda peer: copy_to(0, qk_send.at[peer], qk_land.at[me], peer, peer).start())
+    others(lambda peer: copy_to(1, gv_send.at[peer], gv_land.at[me], peer, peer).start())
+    qk_land[me] = qk_send[me]
+    gv_land[me] = gv_send[me]
+
+    def find_stored(block, carry):
+        where = jnp.int32(0)
+        for stored in range(ring):
+            where = jnp.where(ids_ref[stored] == block, jnp.int32(stored), where)
+        stored_of[block] = where
+        return carry
+
+    lax.fori_loop(0, ring, find_stored, 0)
+
+    def find_slots(query, carry):
+        block = ids_ref[query]
+        for entry in range(near):
+            slot_of[query * near + entry] = stored_of[nbr_ref[block, entry]]
+        return carry
+
+    lax.fori_loop(0, ring, find_slots, 0)
+
+    def find_terms(key, carry):
+        def visit(query, state):
+            count, found = state[0], state[1:]
+            hit = jnp.int32(-1)
+            for entry in range(near):
+                term = query * near + entry
+                hit = jnp.where(slot_of[term] == key, term, hit)
+            found = tuple(
+                jnp.where((count == rank) & (hit >= 0), hit, found[rank]) for rank in range(near)
+            )
+            return (jnp.where(hit >= 0, count + 1, count),) + found
+
+        state = lax.fori_loop(0, ring, visit, (jnp.int32(0),) * (near + 1))
+        for rank in range(near):
+            term_at[key * near + rank] = state[rank + 1]
+        return carry
+
+    lax.fori_loop(0, ring, find_terms, 0)
+
+    others(lambda peer: await_from(0, qk_land.at[peer], peer))
+
+    def turn_keys(block, carry):
+        tile = qk_land[block].astype(jnp.float32)
+        kt_buf[block] = tile.T[width:, :].astype(jnp.bfloat16)
+        return carry
+
+    lax.fori_loop(0, ring, turn_keys, 0)
+
+    nt = (((1,), (1,)), ((), ()))
+    upper = lax.broadcasted_iota(jnp.int32, (rows, 2 * width), 1) >= width
+
+    def as_upper(tile):
+        wide = tile.astype(jnp.float32)
+        moved = jnp.concatenate([wide[:, width:], wide[:, :width]], axis=1)
+        return jnp.where(upper, moved, 0.0).astype(jnp.bfloat16)
+
+    itself = row_index == lax.broadcasted_iota(jnp.int32, (rows, rows), 1)
+
+    def allowed(block, entry):
+        real = row_index < limit - nbr_ref[block, entry] * rows
+        return real | itself if entry == 0 else real
+
+    def weigh(query, carry):
+        block = ids_ref[query]
+        against = as_upper(qk_land[query])
+        keys = jnp.concatenate(
+            [qk_land[slot_of[query * near + entry]] for entry in range(near)], axis=0
+        )
+        scores = lax.dot_general(keys, against, nt, preferred_element_type=jnp.float32)
+        scores = jnp.concatenate(
+            [
+                jnp.where(
+                    allowed(block, entry),
+                    scores[entry * rows : (entry + 1) * rows],
+                    neg_fill,
+                )
+                for entry in range(near)
+            ],
+            axis=0,
+        )
+        work[...] = scores
+        largest = jnp.max(scores, axis=0, keepdims=True)
+        grown = jnp.exp(work[...] - largest)
+        prob_wide[query] = grown
+        shrink = 1.0 / jnp.sum(grown, axis=0, keepdims=True)
+        prob = prob_wide[query] * shrink
+        prob_wide[query] = prob
+        prob_low[pl.ds(query * near, near)] = prob.astype(jnp.bfloat16).reshape(near, rows, rows)
+        return carry
+
+    lax.fori_loop(0, ring, weigh, 0)
+
+    def hand_out(kind, block, tile):
+        out_send[kind, block] = tile
+
+        @pl.when(block != me)
+        def _():
+            copy_to(
+                2 + kind, out_send.at[kind, block], out_land.at[kind, me], block, block
+            ).start()
+
+        @pl.when(block == me)
+        def _():
+            out_land[kind, me] = tile
+
+    def fold(tile):
+        return jnp.concatenate([tile[: rows // 2, :width], tile[rows // 2 :, :width]], axis=1)
+
+    def key_terms(kind, weights, tiles):
+        def one(key, carry):
+            terms = [term_at[key * near + rank] for rank in range(near)]
+            left = jnp.concatenate([weights[term] for term in terms], axis=1)
+            right = jnp.concatenate([tiles[lax.div(term, near)] for term in terms], axis=0)
+            total = jnp.dot(left, right, preferred_element_type=jnp.float32)
+            hand_out(kind, key, fold(total).astype(jnp.bfloat16))
+            return carry
+
+        lax.fori_loop(0, ring, one, 0)
+
+    others(lambda peer: await_from(1, gv_land.at[peer], peer))
+    key_terms(2, prob_low, gv_land)
+
+    def differentiate(query, carry):
+        against = as_upper(gv_land[query])
+        slots = [slot_of[query * near + entry] for entry in range(near)]
+        values = jnp.concatenate([gv_land[slot] for slot in slots], axis=0)
+        work[...] = lax.dot_general(values, against, nt, preferred_element_type=jnp.float32)
+        delta = jnp.sum(prob_wide[query] * work[...], axis=0, keepdims=True)
+        slope = (prob_wide[query] * (work[...] - delta)).astype(jnp.bfloat16)
+        dscores[pl.ds(query * near, near)] = slope.reshape(near, rows, rows)
+        turned = jnp.concatenate([kt_buf[slot] for slot in slots], axis=1)
+        total = jnp.dot(turned, slope, preferred_element_type=jnp.float32) * scale
+        hand_out(0, query, total.astype(jnp.bfloat16))
+        return carry
+
+    lax.fori_loop(0, ring, differentiate, 0)
+    key_terms(1, dscores, qk_land)
+
+    def unfold(kind, out):
+        for pair in range(ring // 2):
+            columns = slice(pair * 2 * width, (pair + 1) * 2 * width)
+            first, second = out_land[kind, 2 * pair], out_land[kind, 2 * pair + 1]
+            out[: rows // 2, columns] = jnp.concatenate(
+                [first[:, :width], second[:, :width]], axis=1
+            )
+            out[rows // 2 :, columns] = jnp.concatenate(
+                [first[:, width:], second[:, width:]], axis=1
+            )
+
+    others(lambda peer: await_from(4, out_land.at[2, peer], peer))
+    unfold(2, gv_out)
+    others(lambda peer: await_from(2, out_land.at[0, peer], peer))
+    for pair in range(ring // 2):
+        columns = slice(pair * 2 * width, (pair + 1) * 2 * width)
+        tile = jnp.concatenate([out_land[0, 2 * pair], out_land[0, 2 * pair + 1]], axis=0)
+        gq_out[:, columns] = tile.astype(jnp.float32).T.astype(jnp.bfloat16)
+    others(lambda peer: await_from(3, out_land.at[1, peer], peer))
+    unfold(1, gk_out)
+
+    others(lambda peer: copy_to(0, qk_send.at[peer], qk_land.at[me], peer, peer).wait_send())
+    others(lambda peer: copy_to(1, gv_send.at[peer], gv_land.at[me], peer, peer).wait_send())
+    for kind in range(3):
+        others(
+            lambda peer: copy_to(
+                2 + kind, out_send.at[kind, peer], out_land.at[kind, me], peer, peer
+            ).wait_send()
+        )
+
+
+def per_head_device(
+    ring, blk_count, queries, keys_in, values, d_out, token_count, block_ids, neighbours
+):
+    rows, features = queries.shape
+    near = neighbours.shape[1]
+    tile = (rows, 2 * HD)
+    low = jnp.bfloat16
+    smem = pl.BlockSpec(memory_space=pltpu.SMEM)
+    vmem = pl.BlockSpec(memory_space=pltpu.VMEM)
+    return pl.pallas_call(
+        functools.partial(head_kernel, ring, blk_count, near),
+        out_shape=[jax.ShapeDtypeStruct((rows, features), low)] * 3,
+        in_specs=[smem] * 3 + [vmem] * 4,
+        out_specs=[vmem] * 3,
+        scratch_shapes=[
+            pltpu.VMEM((ring,) + tile, low),
+            pltpu.VMEM((ring,) + tile, low),
+            pltpu.VMEM((ring,) + tile, low),
+            pltpu.VMEM((ring,) + tile, low),
+            pltpu.VMEM((ring, HD, rows), low),
+            pltpu.VMEM((near * rows, rows), jnp.float32),
+            pltpu.VMEM((ring, near * rows, rows), jnp.float32),
+            pltpu.VMEM((ring * near, rows, rows), low),
+            pltpu.VMEM((ring * near, rows, rows), low),
+            pltpu.VMEM((3, ring, HD, rows), low),
+            pltpu.VMEM((3, ring, HD, rows), low),
+            pltpu.SMEM((ring,), jnp.int32),
+            pltpu.SMEM((ring * near,), jnp.int32),
+            pltpu.SMEM((ring * near,), jnp.int32),
+            pltpu.SemaphoreType.DMA((5, ring)),
+            pltpu.SemaphoreType.DMA((5, ring)),
+        ],
+        compiler_params=pltpu.CompilerParams(
+            collective_id=0, has_side_effects=True, vmem_limit_bytes=48 * 1024 * 1024
+        ),
+        cost_estimate=pl.CostEstimate(
+            flops=10 * ring * near * rows * rows * HD,
+            bytes_accessed=14 * rows * features,
+            transcendentals=ring * near * rows * rows,
+        ),
+    )(token_count, block_ids, neighbours, queries, keys_in, values, d_out)
+
+
+def route(mesh, queries, *rest):
+    rows, features = queries.shape
+    ring = mesh.shape["head"] * mesh.shape["blk"]
+    if rows == BLK and features == ring * HD and 2 * HD == BLK:
+        return tuple(per_head_device(ring, mesh.shape["blk"], queries, *rest))
+    return per_device(queries, *rest)
+
+
 def solution(mesh):
     return jax.shard_map(
-        per_device,
+        functools.partial(route, mesh),
         mesh=mesh,
         in_specs=(
             P(("bend", "head", "blk"), None),

time: 179 us -> 70.9 us (0.40)
  Pallas kernels: 0 us -> 62.7 us
  waiting for transfers between devices: 42.2 us -> 0 us
  matrix products: 33.8 us -> 0 us
  other arithmetic: 29.5 us -> 0 us
  starting transfers between devices: 24.9 us -> 0 us
  local copies, waits for them, and re-layouts: 20.2 us -> 6.6 us
  between operations: 14.9 us -> 1.33 us
  blocking collectives: 12.1 us -> 0 us
    pallas_call x0 -> x1, Pallas kernels: none -> 62.7 us  [per_head_device(): pl.pallas_call(functools.partial(head_kernel, ring, blk_count, near), out...]
    dot_general x20 -> x0, matrix products: 33.8 us -> none  [the longest x4 11.1 us: attend_all(): jnp.einsum('gqnk,gqf->gnkf', prob_low, grad_head, preferred_element_type=...]
    all_to_all x6 -> x0, starting transfers between devices: 24.6 us -> none  [the longest x1 6.32 us: per_device(): lax.all_to_all(keys_in, 'head', split_axis=1, concat_axis=0, tiled=True)]
    all_gather x2 -> x0, waiting for transfers between devices: 18.8 us -> none  [the longest x1 18.7 us: per_device(): lax.all_gather(key_rows, 'blk', axis=0, tiled=True)]
    scatter-add x2 -> x0, other arithmetic: 18.2 us -> none  [the longest x1 9.11 us: summed_step(): running[0].at[flat_slots]]
    all_to_all x6 -> x0, waiting for transfers between devices: 17.7 us -> none  [the longest x1 5.89 us: per_device(): lax.all_to_all(key_grad_rows, 'head', split_axis=0, concat_axis=1, tiled=...]
    all_to_all x1 -> x0, blocking collectives: 12.1 us -> none  [per_device(): lax.all_to_all(query_grad_rows, 'head', split_axis=0, concat_axis=1, tile...]
    convert_element_type x3 -> x0, other arithmetic: 6.42 us -> none  [the longest x1 4.22 us: attend_all(): grad_scores = (probability * (grad_probs - row_delta)).astype(jnp.bfloat16)]
  transfers between devices with their start and end apart: 10 -> 0, of which waited for: 7 -> 0; matrix products, arithmetic and copies ran while one was open for 43% -> 0% of each run, Pallas kernels for 0% -> 0%
where the time goes in v1:
time: 70.9 us; the launch traced here: 70.6 us
  Pallas kernels  62.7 us (88%)
  local copies, waits for them, and re-layouts  6.6 us (9%)
  between operations  1.33 us (2%)
    pallas_call x1, Pallas kernels, per_head_device(): pl.pallas_call(functools.partial(head_kernel, ring, blk_count, near), out...  62.7 us
    unnamed x15, local copies, waits for them, and re-layouts  6.6 us

profile of v1, /device:TPU:0, one launch (start us, length us, event | category | flops | bytes accessed | tf_op | source)
XLA Modules:
  0.0 70.6 jit_solution(17932853573865609336)
XLA Ops:
  0.6 0.0 copy-start.5
  1.3 0.0 copy-done.5
  1.3 0.0 copy-start
  1.3 0.9 %copy-done = bf16[128,1024]{1,0:T(8,128)(2,1)S(1)} copy-done((bf16[128,1024]{1,0:T(8,128)(2,1)S(1)}, bf16[128,1024]{1,0:T(8,128)(2,1)}, u32[]{:S(2)}) %copy-start) | copy-done | bytes 262168
  2.3 0.0 copy-start.1
  2.3 0.9 %copy-done.1 = bf16[128,1024]{1,0:T(8,128)(2,1)S(1)} copy-done((bf16[128,1024]{1,0:T(8,128)(2,1)S(1)}, bf16[128,1024]{1,0:T(8,128)(2,1)}, u32[]{:S(2)}) %copy-start.1) | copy-done | bytes 262168
  3.2 0.0 copy-start.2
  3.2 0.9 %copy-done.2 = bf16[128,1024]{1,0:T(8,128)(2,1)S(1)} copy-done((bf16[128,1024]{1,0:T(8,128)(2,1)S(1)}, bf16[128,1024]{1,0:T(8,128)(2,1)}, u32[]{:S(2)}) %copy-start.2) | copy-done | bytes 262168
  4.2 0.0 copy-start.3
  4.2 0.9 %copy-done.3 = bf16[128,1024]{1,0:T(8,128)(2,1)S(1)} copy-done((bf16[128,1024]{1,0:T(8,128)(2,1)S(1)}, bf16[128,1024]{1,0:T(8,128)(2,1)}, u32[]{:S(2)}) %copy-start.3) | copy-done | bytes 262168
  5.1 0.0 copy-start.4
  5.1 0.7 copy-done.4
  5.8 62.7 %shard_map.94 = (bf16[128,1024]{1,0:T(8,128)(2,1)S(1)}, bf16[128,1024]{1,0:T(8,128)(2,1)S(1)}, bf16[128,1024]{1,0:T(8,128)(2,1)S(1)}) custom-call(s32[1]{0:T(128)S(6)} %copy.13.limit_ref, s32[16]{0:T(128)S(1)} %copy-done.5, s32[16,10]{1,0:T(8,128)S(1)} %copy-done.4, bf16[128,1024]{1,0:T(8,128)(2,1)S(1)} %copy-done, bf16[128,1024]{1,0:T(8,128)(2,1)S(1)} %copy-done.1, ...), custom_call_target="tpu_custom_call" | custom-call | flops 1677721600 | bytes 1835008 | tf_op jit(solution)/shard_map/pallas_call | solution.py:473
  68.5 0.7 copy.14
  69.2 0.7 copy.15
  69.9 0.7 copy.16
Async XLA Ops:
  0.6 0.7 copy-start.5
  1.3 1.0 %copy-start = (bf16[128,1024]{1,0:T(8,128)(2,1)S(1)}, bf16[128,1024]{1,0:T(8,128)(2,1)}, u32[]{:S(2)}) copy-start(bf16[128,1024]{1,0:T(8,128)(2,1)} %q_ref.1) | copy-start | bytes 786436
  2.3 0.9 %copy-start.1 = (bf16[128,1024]{1,0:T(8,128)(2,1)S(1)}, bf16[128,1024]{1,0:T(8,128)(2,1)}, u32[]{:S(2)}) copy-start(bf16[128,1024]{1,0:T(8,128)(2,1)} %k_ref.1) | copy-start | bytes 786436
  3.2 0.9 %copy-start.2 = (bf16[128,1024]{1,0:T(8,128)(2,1)S(1)}, bf16[128,1024]{1,0:T(8,128)(2,1)}, u32[]{:S(2)}) copy-start(bf16[128,1024]{1,0:T(8,128)(2,1)} %v_ref.1) | copy-start | bytes 786436
  4.2 0.9 %copy-start.3 = (bf16[128,1024]{1,0:T(8,128)(2,1)S(1)}, bf16[128,1024]{1,0:T(8,128)(2,1)}, u32[]{:S(2)}) copy-start(bf16[128,1024]{1,0:T(8,128)(2,1)} %g_ref.1) | copy-start | bytes 786436
  5.1 0.7 copy-start.4

commit v2 on v1

--- a/solution.py
+++ b/solution.py
@@ -207,13 +207,17 @@
     limit_ref,
     ids_ref,
     nbr_ref,
+    q_hbm,
+    k_hbm,
+    v_hbm,
+    g_hbm,
+    gq_out,
+    gk_out,
+    gv_out,
     q_ref,
     k_ref,
     v_ref,
     g_ref,
-    gq_out,
-    gk_out,
-    gv_out,
     qk_send,
     gv_send,
     qk_land,
@@ -228,6 +232,7 @@
     stored_of,
     slot_of,
     term_at,
+    load_sem,
     send_sem,
     recv_sem,
 ):
@@ -267,6 +272,14 @@
 
         lax.fori_loop(1, ring, step, 0)
 
+    sources = ((q_hbm, q_ref), (k_hbm, k_ref), (g_hbm, g_ref), (v_hbm, v_ref))
+    loads = [
+        pltpu.make_async_copy(source, held, load_sem.at[index])
+        for index, (source, held) in enumerate(sources)
+    ]
+    for load in loads:
+        load.start()
+
     barrier = pltpu.get_barrier_semaphore()
     others(
         lambda peer: pl.semaphore_signal(
@@ -276,6 +289,8 @@
 
     row_index = lax.broadcasted_iota(jnp.int32, (rows, 2 * width), 0)
 
+    for load in loads:
+        load.wait()
     my_limit = limit - ids_ref[me] * rows
     for pair in range(ring // 2):
         columns = slice(pair * 2 * width, (pair + 1) * 2 * width)
@@ -314,19 +329,17 @@
 
     def find_terms(key, carry):
         def visit(query, state):
-            count, found = state[0], state[1:]
             hit = jnp.int32(-1)
             for entry in range(near):
                 term = query * near + entry
                 hit = jnp.where(slot_of[term] == key, term, hit)
-            found = tuple(
-                jnp.where((count == rank) & (hit >= 0), hit, found[rank]) for rank in range(near)
+            return tuple(
+                jnp.where(hit >= 0, older, held) for older, held in zip((hit,) + state, state)
             )
-            return (jnp.where(hit >= 0, count + 1, count),) + found
-
-        state = lax.fori_loop(0, ring, visit, (jnp.int32(0),) * (near + 1))
+
+        state = lax.fori_loop(0, ring, visit, (jnp.int32(0),) * near)
         for rank in range(near):
-            term_at[key * near + rank] = state[rank + 1]
+            term_at[key * near + rank] = state[rank]
         return carry
 
     lax.fori_loop(0, ring, find_terms, 0)
@@ -401,7 +414,8 @@
         return jnp.concatenate([tile[: rows // 2, :width], tile[rows // 2 :, :width]], axis=1)
 
     def key_terms(kind, weights, tiles):
-        def one(key, carry):
+        def one(step, carry):
+            key = lax.rem(me + 1 + step, ring)
             terms = [term_at[key * near + rank] for rank in range(near)]
             left = jnp.concatenate([weights[term] for term in terms], axis=1)
             right = jnp.concatenate([tiles[lax.div(term, near)] for term in terms], axis=0)
@@ -414,7 +428,8 @@
     others(lambda peer: await_from(1, gv_land.at[peer], peer))
     key_terms(2, prob_low, gv_land)
 
-    def differentiate(query, carry):
+    def differentiate(step, carry):
+        query = lax.rem(me + 1 + step, ring)
         against = as_upper(gv_land[query])
         slots = [slot_of[query * near + entry] for entry in range(near)]
         values = jnp.concatenate([gv_land[slot] for slot in slots], axis=0)
@@ -473,9 +488,10 @@
     return pl.pallas_call(
         functools.partial(head_kernel, ring, blk_count, near),
         out_shape=[jax.ShapeDtypeStruct((rows, features), low)] * 3,
-        in_specs=[smem] * 3 + [vmem] * 4,
+        in_specs=[smem] * 3 + [pl.BlockSpec(memory_space=pltpu.HBM)] * 4,
         out_specs=[vmem] * 3,
-        scratch_shapes=[
+        scratch_shapes=[pltpu.VMEM((rows, features), low)] * 4
+        + [
             pltpu.VMEM((ring,) + tile, low),
             pltpu.VMEM((ring,) + tile, low),
             pltpu.VMEM((ring,) + tile, low),
@@ -490,6 +506,7 @@
             pltpu.SMEM((ring,), jnp.int32),
             pltpu.SMEM((ring * near,), jnp.int32),
             pltpu.SMEM((ring * near,), jnp.int32),
+            pltpu.SemaphoreType.DMA((4,)),
             pltpu.SemaphoreType.DMA((5, ring)),
             pltpu.SemaphoreType.DMA((5, ring)),
         ],

time: 70.9 us -> 71.6 us (level)
  no operation moved by 1% of the time
where the time goes in v2:
time: 71.6 us; the launch traced here: 71.3 us
  Pallas kernels  63.4 us (89%)
  local copies, waits for them, and re-layouts  6.6 us (9%)
  between operations  1.33 us (2%)
    pallas_call x1, Pallas kernels, per_head_device(): pl.pallas_call(functools.partial(head_kernel, ring, blk_count, near), out...  63.4 us
    unnamed x15, local copies, waits for them, and re-layouts  6.6 us

profile of v2, /device:TPU:0, one launch (start us, length us, event | category | flops | bytes accessed | tf_op | source)
XLA Modules:
  0.0 71.3 jit_solution(6337495129755236250)
XLA Ops:
  0.6 0.0 copy-start.5
  1.3 0.0 copy-done.5
  1.3 0.0 copy-start
  1.3 0.9 %copy-done = bf16[128,1024]{1,0:T(8,128)(2,1)S(1)} copy-done((bf16[128,1024]{1,0:T(8,128)(2,1)S(1)}, bf16[128,1024]{1,0:T(8,128)(2,1)}, u32[]{:S(2)}) %copy-start) | copy-done | bytes 262168
  2.3 0.0 copy-start.1
  2.3 0.9 %copy-done.1 = bf16[128,1024]{1,0:T(8,128)(2,1)S(1)} copy-done((bf16[128,1024]{1,0:T(8,128)(2,1)S(1)}, bf16[128,1024]{1,0:T(8,128)(2,1)}, u32[]{:S(2)}) %copy-start.1) | copy-done | bytes 262168
  3.2 0.0 copy-start.2
  3.2 0.9 %copy-done.2 = bf16[128,1024]{1,0:T(8,128)(2,1)S(1)} copy-done((bf16[128,1024]{1,0:T(8,128)(2,1)S(1)}, bf16[128,1024]{1,0:T(8,128)(2,1)}, u32[]{:S(2)}) %copy-start.2) | copy-done | bytes 262168
  4.2 0.0 copy-start.3
  4.2 0.9 %copy-done.3 = bf16[128,1024]{1,0:T(8,128)(2,1)S(1)} copy-done((bf16[128,1024]{1,0:T(8,128)(2,1)S(1)}, bf16[128,1024]{1,0:T(8,128)(2,1)}, u32[]{:S(2)}) %copy-start.3) | copy-done | bytes 262168
  5.1 0.0 copy-start.4
  5.1 0.7 copy-done.4
  5.8 63.4 %shard_map.94 = (bf16[128,1024]{1,0:T(8,128)(2,1)S(1)}, bf16[128,1024]{1,0:T(8,128)(2,1)S(1)}, bf16[128,1024]{1,0:T(8,128)(2,1)S(1)}) custom-call(s32[1]{0:T(128)S(6)} %copy.13.limit_ref, s32[16]{0:T(128)S(1)} %copy-done.5, s32[16,10]{1,0:T(8,128)S(1)} %copy-done.4, bf16[128,1024]{1,0:T(8,128)(2,1)S(1)} %copy-done, bf16[128,1024]{1,0:T(8,128)(2,1)S(1)} %copy-done.1, ...), custom_call_target="tpu_custom_call" | custom-call | flops 1677721600 | bytes 1835008 | tf_op jit(solution)/shard_map/pallas_call | solution.py:488
  69.2 0.7 copy.14
  69.9 0.7 copy.15
  70.6 0.7 copy.16
Async XLA Ops:
  0.6 0.7 copy-start.5
  1.3 1.0 %copy-start = (bf16[128,1024]{1,0:T(8,128)(2,1)S(1)}, bf16[128,1024]{1,0:T(8,128)(2,1)}, u32[]{:S(2)}) copy-start(bf16[128,1024]{1,0:T(8,128)(2,1)} %q_hbm.1) | copy-start | bytes 786436
  2.3 0.9 %copy-start.1 = (bf16[128,1024]{1,0:T(8,128)(2,1)S(1)}, bf16[128,1024]{1,0:T(8,128)(2,1)}, u32[]{:S(2)}) copy-start(bf16[128,1024]{1,0:T(8,128)(2,1)} %k_hbm.1) | copy-start | bytes 786436
  3.2 0.9 %copy-start.2 = (bf16[128,1024]{1,0:T(8,128)(2,1)S(1)}, bf16[128,1024]{1,0:T(8,128)(2,1)}, u32[]{:S(2)}) copy-start(bf16[128,1024]{1,0:T(8,128)(2,1)} %v_hbm.1) | copy-start | bytes 786436
  4.2 0.9 %copy-start.3 = (bf16[128,1024]{1,0:T(8,128)(2,1)S(1)}, bf16[128,1024]{1,0:T(8,128)(2,1)}, u32[]{:S(2)}) copy-start(bf16[128,1024]{1,0:T(8,128)(2,1)} %g_hbm.1) | copy-start | bytes 786436
  5.1 0.7 copy-start.4

commit v3 on v2

--- a/solution.py
+++ b/solution.py
@@ -223,8 +223,11 @@
     qk_land,
     gv_land,
     kt_buf,
+    key_biased,
     work,
-    prob_wide,
+    work_next,
+    shrink,
+    shrink_row,
     prob_low,
     dscores,
     out_send,
@@ -346,56 +349,54 @@
 
     others(lambda peer: await_from(0, qk_land.at[peer], peer))
 
+    lane = lax.broadcasted_iota(jnp.int32, (rows, 2 * width), 1)
+    upper = lane >= width
+
     def turn_keys(block, carry):
         tile = qk_land[block].astype(jnp.float32)
         kt_buf[block] = tile.T[width:, :].astype(jnp.bfloat16)
+        real = row_index < limit - ids_ref[block] * rows
+        bias = jnp.where((lane == 0) & ~real, neg_fill, 0.0)
+        key_biased[block] = jnp.where(upper, tile, bias).astype(jnp.bfloat16)
         return carry
 
     lax.fori_loop(0, ring, turn_keys, 0)
 
     nt = (((1,), (1,)), ((), ()))
-    upper = lax.broadcasted_iota(jnp.int32, (rows, 2 * width), 1) >= width
-
-    def as_upper(tile):
+
+    def as_upper(tile, lowest):
         wide = tile.astype(jnp.float32)
         moved = jnp.concatenate([wide[:, width:], wide[:, :width]], axis=1)
-        return jnp.where(upper, moved, 0.0).astype(jnp.bfloat16)
+        return jnp.where(upper, moved, jnp.where(lane == 0, lowest, 0.0)).astype(jnp.bfloat16)
 
     itself = row_index == lax.broadcasted_iota(jnp.int32, (rows, rows), 1)
 
-    def allowed(block, entry):
-        real = row_index < limit - nbr_ref[block, entry] * rows
-        return real | itself if entry == 0 else real
-
-    def weigh(query, carry):
+    def weigh(query, held):
         block = ids_ref[query]
-        against = as_upper(qk_land[query])
+        own = slot_of[query * near]
+        against = as_upper(qk_land[query], 1.0)
         keys = jnp.concatenate(
-            [qk_land[slot_of[query * near + entry]] for entry in range(near)], axis=0
-        )
-        scores = lax.dot_general(keys, against, nt, preferred_element_type=jnp.float32)
-        scores = jnp.concatenate(
-            [
-                jnp.where(
-                    allowed(block, entry),
-                    scores[entry * rows : (entry + 1) * rows],
-                    neg_fill,
-                )
-                for entry in range(near)
-            ],
-            axis=0,
-        )
-        work[...] = scores
-        largest = jnp.max(scores, axis=0, keepdims=True)
-        grown = jnp.exp(work[...] - largest)
-        prob_wide[query] = grown
-        shrink = 1.0 / jnp.sum(grown, axis=0, keepdims=True)
-        prob = prob_wide[query] * shrink
-        prob_wide[query] = prob
-        prob_low[pl.ds(query * near, near)] = prob.astype(jnp.bfloat16).reshape(near, rows, rows)
-        return carry
-
-    lax.fori_loop(0, ring, weigh, 0)
+            [key_biased[slot_of[query * near + entry]] for entry in range(1, near)], axis=0
+        )
+        first = lax.dot_general(
+            qk_land[own], as_upper(qk_land[query], 0.0), nt, preferred_element_type=jnp.float32
+        )
+        real = row_index < limit - block * rows
+        held[:rows] = jnp.where(real | itself, first, neg_fill)
+        held[rows:] = lax.dot_general(keys, against, nt, preferred_element_type=jnp.float32)
+        largest = jnp.max(held[...], axis=0, keepdims=True)
+        grown = jnp.exp(held[...] - largest).astype(jnp.bfloat16)
+        total = jnp.sum(grown.astype(jnp.float32), axis=0, keepdims=True)
+        prob_low[pl.ds(query * near, near)] = grown.reshape(near, rows, rows)
+        shrink[query] = jnp.broadcast_to(1.0 / total, (rows, rows)).T
+        shrink_row[query] = jnp.broadcast_to(1.0 / total, (8, rows))
+
+    def weigh_two(step, carry):
+        weigh(2 * step, work)
+        weigh(2 * step + 1, work_next)
+        return carry
+
+    lax.fori_loop(0, ring // 2, weigh_two, 0)
 
     def hand_out(kind, block, tile):
         out_send[kind, block] = tile
@@ -413,37 +414,63 @@
     def fold(tile):
         return jnp.concatenate([tile[: rows // 2, :width], tile[rows // 2 :, :width]], axis=1)
 
-    def key_terms(kind, weights, tiles):
-        def one(step, carry):
-            key = lax.rem(me + 1 + step, ring)
-            terms = [term_at[key * near + rank] for rank in range(near)]
-            left = jnp.concatenate([weights[term] for term in terms], axis=1)
-            right = jnp.concatenate([tiles[lax.div(term, near)] for term in terms], axis=0)
-            total = jnp.dot(left, right, preferred_element_type=jnp.float32)
-            hand_out(kind, key, fold(total).astype(jnp.bfloat16))
-            return carry
-
-        lax.fori_loop(0, ring, one, 0)
+    def key_terms(weights, tiles, key):
+        terms = [term_at[key * near + rank] for rank in range(near)]
+        left = jnp.concatenate([weights[term] for term in terms], axis=1)
+        right = jnp.concatenate([tiles[lax.div(term, near)] for term in terms], axis=0)
+        total = jnp.dot(left, right, preferred_element_type=jnp.float32)
+        return fold(total).astype(jnp.bfloat16)
 
     others(lambda peer: await_from(1, gv_land.at[peer], peer))
-    key_terms(2, prob_low, gv_land)
-
-    def differentiate(step, carry):
-        query = lax.rem(me + 1 + step, ring)
-        against = as_upper(gv_land[query])
+
+    def scale_grads(block, carry):
+        tile = gv_land[block].astype(jnp.float32)
+        gv_land[block] = jnp.where(upper, tile, tile * shrink[block]).astype(jnp.bfloat16)
+        return carry
+
+    lax.fori_loop(0, ring, scale_grads, 0)
+
+    def differentiate(query, held):
+        against = as_upper(gv_land[query], 0.0)
         slots = [slot_of[query * near + entry] for entry in range(near)]
         values = jnp.concatenate([gv_land[slot] for slot in slots], axis=0)
-        work[...] = lax.dot_general(values, against, nt, preferred_element_type=jnp.float32)
-        delta = jnp.sum(prob_wide[query] * work[...], axis=0, keepdims=True)
-        slope = (prob_wide[query] * (work[...] - delta)).astype(jnp.bfloat16)
+        held[...] = lax.dot_general(values, against, nt, preferred_element_type=jnp.float32)
+        prob = prob_low[pl.ds(query * near, near)].reshape(near * rows, rows)
+        delta = jnp.sum(prob.astype(jnp.float32) * held[...], axis=0, keepdims=True)
+        delta = delta * shrink_row[query][:1]
+        slope = (prob.astype(jnp.float32) * (held[...] - delta)).astype(jnp.bfloat16)
         dscores[pl.ds(query * near, near)] = slope.reshape(near, rows, rows)
         turned = jnp.concatenate([kt_buf[slot] for slot in slots], axis=1)
         total = jnp.dot(turned, slope, preferred_element_type=jnp.float32) * scale
-        hand_out(0, query, total.astype(jnp.bfloat16))
-        return carry
-
-    lax.fori_loop(0, ring, differentiate, 0)
-    key_terms(1, dscores, qk_land)
+        return total.astype(jnp.bfloat16)
+
+    def middle(step, carry):
+        first = lax.rem(me + 1 + 2 * step, ring)
+        second = lax.rem(me + 2 + 2 * step, ring)
+        results = (
+            (0, first, differentiate(first, work)),
+            (2, first, key_terms(prob_low, gv_land, first)),
+            (0, second, differentiate(second, work_next)),
+            (2, second, key_terms(prob_low, gv_land, second)),
+        )
+        for result in results:
+            hand_out(*result)
+        return carry
+
+    lax.fori_loop(0, ring // 2, middle, 0)
+
+    def last(step, carry):
+        first = lax.rem(me + 1 + 2 * step, ring)
+        second = lax.rem(me + 2 + 2 * step, ring)
+        results = (
+            (1, first, key_terms(dscores, qk_land, first)),
+            (1, second, key_terms(dscores, qk_land, second)),
+        )
+        for result in results:
+            hand_out(*result)
+        return carry
+
+    lax.fori_loop(0, ring // 2, last, 0)
 
     def unfold(kind, out):
         for pair in range(ring // 2):
@@ -488,7 +515,7 @@
     return pl.pallas_call(
         functools.partial(head_kernel, ring, blk_count, near),
         out_shape=[jax.ShapeDtypeStruct((rows, features), low)] * 3,
-        in_specs=[smem] * 3 + [pl.BlockSpec(memory_space=pltpu.HBM)] * 4,
+        in_specs=[smem] * 3 + [pl.BlockSpec(memory_space=pl.ANY)] * 4,
         out_specs=[vmem] * 3,
         scratch_shapes=[pltpu.VMEM((rows, features), low)] * 4
         + [
@@ -497,8 +524,11 @@
             pltpu.VMEM((ring,) + tile, low),
             pltpu.VMEM((ring,) + tile, low),
             pltpu.VMEM((ring, HD, rows), low),
+            pltpu.VMEM((ring,) + tile, low),
             pltpu.VMEM((near * rows, rows), jnp.float32),
-            pltpu.VMEM((ring, near * rows, rows), jnp.float32),
+            pltpu.VMEM((near * rows, rows), jnp.float32),
+            pltpu.VMEM((ring, rows, rows), jnp.float32),
+            pltpu.VMEM((ring, 8, rows), jnp.float32),
             pltpu.VMEM((ring * near, rows, rows), low),
             pltpu.VMEM((ring * near, rows, rows), low),
             pltpu.VMEM((3, ring, HD, rows), low),
@@ -511,7 +541,7 @@
             pltpu.SemaphoreType.DMA((5, ring)),
         ],
         compiler_params=pltpu.CompilerParams(
-            collective_id=0, has_side_effects=True, vmem_limit_bytes=48 * 1024 * 1024
+            collective_id=0, has_side_effects=True, vmem_limit_bytes=60 * 1024 * 1024
         ),
         cost_estimate=pl.CostEstimate(
             flops=10 * ring * near * rows * rows * HD,
@@ -524,7 +554,7 @@
 def route(mesh, queries, *rest):
     rows, features = queries.shape
     ring = mesh.shape["head"] * mesh.shape["blk"]
-    if rows == BLK and features == ring * HD and 2 * HD == BLK:
+    if rows == BLK and features == ring * HD and 2 * HD == BLK and ring % 2 == 0:
         return tuple(per_head_device(ring, mesh.shape["blk"], queries, *rest))
     return per_device(queries, *rest)
 

time: 71.6 us -> 60.1 us (0.84)
  Pallas kernels: 63.4 us -> 55.1 us
  local copies, waits for them, and re-layouts: 6.6 us -> 3.46 us
    pallas_call x1, Pallas kernels: 63.4 us -> 55.1 us  [per_head_device(): pl.pallas_call(functools.partial(head_kernel, ring, blk_count, near), out...]
    unnamed x15 -> x7, local copies, waits for them, and re-layouts: 6.6 us -> 3.46 us
where the time goes in v3:
time: 60.1 us; the launch traced here: 59.9 us
  Pallas kernels  55.1 us (92%)
  local copies, waits for them, and re-layouts  3.46 us (6%)
  between operations  1.3 us (2%)
    pallas_call x1, Pallas kernels, per_head_device(): pl.pallas_call(functools.partial(head_kernel, ring, blk_count, near), out...  55.1 us
    unnamed x7, local copies, waits for them, and re-layouts  3.46 us

profile of v3, /device:TPU:0, one launch (start us, length us, event | category | flops | bytes accessed | tf_op | source)
XLA Modules:
  0.0 59.9 jit_solution(9808165407856014871)
XLA Ops:
  1.3 55.1 %shard_map.94 = (bf16[128,1024]{1,0:T(8,128)(2,1)}, bf16[128,1024]{1,0:T(8,128)(2,1)}, bf16[128,1024]{1,0:T(8,128)(2,1)}) custom-call(s32[1]{0:T(128)S(6)} %copy.13.limit_ref, s32[16]{0:T(128)} %ids_ref.1, s32[16,10]{1,0:T(8,128)} %nbr_ref.1, bf16[128,1024]{1,0:T(8,128)(2,1)} %q_hbm.1, bf16[128,1024]{1,0:T(8,128)(2,1)} %k_hbm.1, bf16[128,1024]{1,0:T(8,128)(2,1)} %v_hbm.1, ...), custom_call_target="tpu_custom_call" | custom-call | flops 1677721600 | bytes 1835008 | tf_op jit(solution)/shard_map/pallas_call | solution.py:515
  56.4 0.0 copy-start.1
  56.4 1.7 %copy.14 = bf16[128,1024]{1,0:T(8,128)(2,1)} copy(bf16[128,1024]{1,0:T(8,128)(2,1)} %get-tuple-element.6) | data formatting | bytes 524288
  58.1 0.0 copy-done.1
  58.1 0.0 copy-start
  58.1 0.7 %copy.15 = bf16[128,1024]{1,0:T(8,128)(2,1)} copy(bf16[128,1024]{1,0:T(8,128)(2,1)S(1)} %copy-done.1) | data formatting | bytes 524288
  58.8 0.3 copy-done
  59.2 0.7 %copy.16 = bf16[128,1024]{1,0:T(8,128)(2,1)} copy(bf16[128,1024]{1,0:T(8,128)(2,1)S(1)} %copy-done) | data formatting | bytes 524288
Async XLA Ops:
  56.4 1.7 %copy-start.1 = (bf16[128,1024]{1,0:T(8,128)(2,1)S(1)}, bf16[128,1024]{1,0:T(8,128)(2,1)}, u32[]{:S(2)}) copy-start(bf16[128,1024]{1,0:T(8,128)(2,1)} %get-tuple-element.7) | copy-start | bytes 786436
  58.1 1.0 %copy-start = (bf16[128,1024]{1,0:T(8,128)(2,1)S(1)}, bf16[128,1024]{1,0:T(8,128)(2,1)}, u32[]{:S(2)}) copy-start(bf16[128,1024]{1,0:T(8,128)(2,1)} %get-tuple-element.8) | copy-start | bytes 786436

commit v4 on v3

--- a/solution.py
+++ b/solution.py
@@ -309,7 +309,6 @@
 
     pl.semaphore_wait(barrier, ring - 1)
     others(lambda peer: copy_to(0, qk_send.at[peer], qk_land.at[me], peer, peer).start())
-    others(lambda peer: copy_to(1, gv_send.at[peer], gv_land.at[me], peer, peer).start())
     qk_land[me] = qk_send[me]
     gv_land[me] = gv_send[me]
 
@@ -347,6 +346,8 @@
 
     lax.fori_loop(0, ring, find_terms, 0)
 
+    others(lambda peer: copy_to(0, qk_send.at[peer], qk_land.at[me], peer, peer).wait_send())
+    others(lambda peer: copy_to(1, gv_send.at[peer], gv_land.at[me], peer, peer).start())
     others(lambda peer: await_from(0, qk_land.at[peer], peer))
 
     lane = lax.broadcasted_iota(jnp.int32, (rows, 2 * width), 1)
@@ -493,7 +494,6 @@
     others(lambda peer: await_from(3, out_land.at[1, peer], peer))
     unfold(1, gk_out)
 
-    others(lambda peer: copy_to(0, qk_send.at[peer], qk_land.at[me], peer, peer).wait_send())
     others(lambda peer: copy_to(1, gv_send.at[peer], gv_land.at[me], peer, peer).wait_send())
     for kind in range(3):
         others(

time: 60.1 us -> 61.4 us (1.022)
  Pallas kernels: 55.1 us -> 56.4 us
    pallas_call x1, Pallas kernels: 55.1 us -> 56.4 us  [per_head_device(): pl.pallas_call(functools.partial(head_kernel, ring, blk_count, near), out...]
where the time goes in v4:
time: 61.4 us; the launch traced here: 61.1 us
  Pallas kernels  56.4 us (92%)
  local copies, waits for them, and re-layouts  3.46 us (6%)
  between operations  1.3 us (2%)
    pallas_call x1, Pallas kernels, per_head_device(): pl.pallas_call(functools.partial(head_kernel, ring, blk_count, near), out...  56.4 us
    unnamed x7, local copies, waits for them, and re-layouts  3.46 us

profile of v4, /device:TPU:0, one launch (start us, length us, event | category | flops | bytes accessed | tf_op | source)
XLA Modules:
  0.0 61.1 jit_solution(252191378510705317)
XLA Ops:
  1.3 56.4 %shard_map.94 = (bf16[128,1024]{1,0:T(8,128)(2,1)}, bf16[128,1024]{1,0:T(8,128)(2,1)}, bf16[128,1024]{1,0:T(8,128)(2,1)}) custom-call(s32[1]{0:T(128)S(6)} %copy.13.limit_ref, s32[16]{0:T(128)} %ids_ref.1, s32[16,10]{1,0:T(8,128)} %nbr_ref.1, bf16[128,1024]{1,0:T(8,128)(2,1)} %q_hbm.1, bf16[128,1024]{1,0:T(8,128)(2,1)} %k_hbm.1, bf16[128,1024]{1,0:T(8,128)(2,1)} %v_hbm.1, ...), custom_call_target="tpu_custom_call" | custom-call | flops 1677721600 | bytes 1835008 | tf_op jit(solution)/shard_map/pallas_call | solution.py:515
  57.7 0.0 copy-start.1
  57.7 1.7 %copy.14 = bf16[128,1024]{1,0:T(8,128)(2,1)} copy(bf16[128,1024]{1,0:T(8,128)(2,1)} %get-tuple-element.6) | data formatting | bytes 524288
  59.4 0.0 copy-done.1
  59.4 0.0 copy-start
  59.4 0.7 %copy.15 = bf16[128,1024]{1,0:T(8,128)(2,1)} copy(bf16[128,1024]{1,0:T(8,128)(2,1)S(1)} %copy-done.1) | data formatting | bytes 524288
  60.1 0.3 copy-done
  60.4 0.7 %copy.16 = bf16[128,1024]{1,0:T(8,128)(2,1)} copy(bf16[128,1024]{1,0:T(8,128)(2,1)S(1)} %copy-done) | data formatting | bytes 524288
Async XLA Ops:
  57.7 1.7 %copy-start.1 = (bf16[128,1024]{1,0:T(8,128)(2,1)S(1)}, bf16[128,1024]{1,0:T(8,128)(2,1)}, u32[]{:S(2)}) copy-start(bf16[128,1024]{1,0:T(8,128)(2,1)} %get-tuple-element.7) | copy-start | bytes 786436
  59.4 1.0 %copy-start = (bf16[128,1024]{1,0:T(8,128)(2,1)S(1)}, bf16[128,1024]{1,0:T(8,128)(2,1)}, u32[]{:S(2)}) copy-start(bf16[128,1024]{1,0:T(8,128)(2,1)} %get-tuple-element.8) | copy-start | bytes 786436

commit v5 on v3

--- a/solution.py
+++ b/solution.py
@@ -226,6 +226,8 @@
     key_biased,
     work,
     work_next,
+    work_third,
+    work_fourth,
     shrink,
     shrink_row,
     prob_low,
@@ -391,12 +393,15 @@
         shrink[query] = jnp.broadcast_to(1.0 / total, (rows, rows)).T
         shrink_row[query] = jnp.broadcast_to(1.0 / total, (8, rows))
 
-    def weigh_two(step, carry):
-        weigh(2 * step, work)
-        weigh(2 * step + 1, work_next)
-        return carry
-
-    lax.fori_loop(0, ring // 2, weigh_two, 0)
+    buffers = (work, work_next, work_third, work_fourth)
+    group = len(buffers)
+
+    def weigh_group(step, carry):
+        for index, held in enumerate(buffers):
+            weigh(group * step + index, held)
+        return carry
+
+    lax.fori_loop(0, ring // group, weigh_group, 0)
 
     def hand_out(kind, block, tile):
         out_send[kind, block] = tile
@@ -460,17 +465,13 @@
     lax.fori_loop(0, ring // 2, middle, 0)
 
     def last(step, carry):
-        first = lax.rem(me + 1 + 2 * step, ring)
-        second = lax.rem(me + 2 + 2 * step, ring)
-        results = (
-            (1, first, key_terms(dscores, qk_land, first)),
-            (1, second, key_terms(dscores, qk_land, second)),
-        )
-        for result in results:
-            hand_out(*result)
-        return carry
-
-    lax.fori_loop(0, ring // 2, last, 0)
+        keys = [lax.rem(me + 1 + group * step + index, ring) for index in range(group)]
+        results = [key_terms(dscores, qk_land, key) for key in keys]
+        for key, result in zip(keys, results):
+            hand_out(1, key, result)
+        return carry
+
+    lax.fori_loop(0, ring // group, last, 0)
 
     def unfold(kind, out):
         for pair in range(ring // 2):
@@ -527,6 +528,8 @@
             pltpu.VMEM((ring,) + tile, low),
             pltpu.VMEM((near * rows, rows), jnp.float32),
             pltpu.VMEM((near * rows, rows), jnp.float32),
+            pltpu.VMEM((near * rows, rows), jnp.float32),
+            pltpu.VMEM((near * rows, rows), jnp.float32),
             pltpu.VMEM((ring, rows, rows), jnp.float32),
             pltpu.VMEM((ring, 8, rows), jnp.float32),
             pltpu.VMEM((ring * near, rows, rows), low),
@@ -554,7 +557,7 @@
 def route(mesh, queries, *rest):
     rows, features = queries.shape
     ring = mesh.shape["head"] * mesh.shape["blk"]
-    if rows == BLK and features == ring * HD and 2 * HD == BLK and ring % 2 == 0:
+    if rows == BLK and features == ring * HD and 2 * HD == BLK and ring % 4 == 0:
         return tuple(per_head_device(ring, mesh.shape["blk"], queries, *rest))
     return per_device(queries, *rest)
 

time: 60.1 us -> 58.8 us (0.978)
  Pallas kernels: 55.1 us -> 53.3 us
    pallas_call x1, Pallas kernels: 55.1 us -> 53.3 us  [per_head_device(): pl.pallas_call(functools.partial(head_kernel, ring, blk_count, near), out...]
where the time goes in v5:
time: 58.8 us; the launch traced here: 58.1 us
  Pallas kernels  53.3 us (91%)
  local copies, waits for them, and re-layouts  3.46 us (6%)
  between operations  1.3 us (2%)
    pallas_call x1, Pallas kernels, per_head_device(): pl.pallas_call(functools.partial(head_kernel, ring, blk_count, near), out...  53.3 us
    unnamed x7, local copies, waits for them, and re-layouts  3.46 us

profile of v5, /device:TPU:0, one launch (start us, length us, event | category | flops | bytes accessed | tf_op | source)
XLA Modules:
  0.0 58.1 jit_solution(8891096233676683570)
XLA Ops:
  1.3 53.3 %shard_map.94 = (bf16[128,1024]{1,0:T(8,128)(2,1)}, bf16[128,1024]{1,0:T(8,128)(2,1)}, bf16[128,1024]{1,0:T(8,128)(2,1)}) custom-call(s32[1]{0:T(128)S(6)} %copy.13.limit_ref, s32[16]{0:T(128)} %ids_ref.1, s32[16,10]{1,0:T(8,128)} %nbr_ref.1, bf16[128,1024]{1,0:T(8,128)(2,1)} %q_hbm.1, bf16[128,1024]{1,0:T(8,128)(2,1)} %k_hbm.1, bf16[128,1024]{1,0:T(8,128)(2,1)} %v_hbm.1, ...), custom_call_target="tpu_custom_call" | custom-call | flops 1677721600 | bytes 1835008 | tf_op jit(solution)/shard_map/pallas_call | solution.py:516
  54.6 0.0 copy-start.1
  54.6 1.7 %copy.14 = bf16[128,1024]{1,0:T(8,128)(2,1)} copy(bf16[128,1024]{1,0:T(8,128)(2,1)} %get-tuple-element.6) | data formatting | bytes 524288
  56.3 0.0 copy-done.1
  56.4 0.0 copy-start
  56.4 0.7 %copy.15 = bf16[128,1024]{1,0:T(8,128)(2,1)} copy(bf16[128,1024]{1,0:T(8,128)(2,1)S(1)} %copy-done.1) | data formatting | bytes 524288
  57.1 0.3 copy-done
  57.4 0.7 %copy.16 = bf16[128,1024]{1,0:T(8,128)(2,1)} copy(bf16[128,1024]{1,0:T(8,128)(2,1)S(1)} %copy-done) | data formatting | bytes 524288
Async XLA Ops:
  54.6 1.7 %copy-start.1 = (bf16[128,1024]{1,0:T(8,128)(2,1)S(1)}, bf16[128,1024]{1,0:T(8,128)(2,1)}, u32[]{:S(2)}) copy-start(bf16[128,1024]{1,0:T(8,128)(2,1)} %get-tuple-element.7) | copy-start | bytes 786436
  56.4 1.0 %copy-start = (bf16[128,1024]{1,0:T(8,128)(2,1)S(1)}, bf16[128,1024]{1,0:T(8,128)(2,1)}, u32[]{:S(2)}) copy-start(bf16[128,1024]{1,0:T(8,128)(2,1)} %get-tuple-element.8) | copy-start | bytes 786436
